TPU v7x, 32 devices: a whole 2x2x4 slice. The times are simulated.
32 devices in a mesh: lat: 4 (over z), ord: 2 (over core), orb: 4 (over y, x).
Axes of the slice: x: 2, y: 2, z: 4, core: 2. Of those that a mesh axis runs over, the one named last changes fastest.
Arguments:
- anomaly: bfloat16 [2, 64, 4320], P(None, 'lat'), may hold values from -6 to 6
- row_weight: float32 [2, 64], replicated, may hold values from 0.2 to 1
- panel: bfloat16 [4, 4, 64, 2, 640], P('orb', None, 'lat', 'ord'), may hold values from -0.5 to 0.5
- order_value: int32 [4, 4], P('orb'), may hold values from 0 to 2159
- deg_first: int32 [4, 4], P('orb', 'lat'), may hold values from 0 to 2190
- sat_rows: bfloat16 [8192, 256], P(('lat', 'ord', 'orb')), may hold values from -0.25 to 0.25
- sat_slot: int32 [8192, 1], P(('lat', 'ord', 'orb')), may hold values from 0 to 15; in each aligned block of 256 rows (0 to 255, 256 to 511, ...) at most 32 rows name the same one
Outputs:
- normals: float32 [4, 4, 2, 640, 2, 640], P('orb', 'lat', 'ord')
- right_side: float32 [4, 4, 2, 2, 640], P('orb', 'lat', None, 'ord')
Inputs may be any that keep to these rules, and one draw needn't show every extreme that they name: `sat_slot`: among the 256 rows of one device no order slot appears more than 32 times.
All inputs are finite; a program needn't handle non-finite values.
Results may differ from a plain program's by a relative error of at most 0.0029.
Values may be sent and summed in bfloat16 or wider, within the bound.
A program may use at most 64 MiB of HBM per device.

v0:
```python
import math

import jax
import jax.numpy as jnp
from jax import lax
from jax.sharding import PartitionSpec as P

LMAX = 2190


def window_flags(first_degree, order_now, half_count):
    parity_col = (
        jnp.arange(2, dtype=jnp.int32)[:, None]
        + 2 * jnp.arange(half_count, dtype=jnp.int32)[None, :]
    )
    degree = first_degree[:, None, None] + parity_col[None]
    live_flags = (degree <= LMAX).astype(jnp.float32)
    parity = (degree + order_now[:, None, None]) % 2
    return (live_flags, 1.0 - 2.0 * parity.astype(jnp.float32))


def fourier_table(order_row, length):
    sample = jnp.arange(length, dtype=jnp.int32)
    phase_index = sample[:, None] * order_row[None, :] % length
    angle_value = phase_index.astype(jnp.float32) * (2.0 * math.pi / length)
    return jnp.concatenate([jnp.cos(angle_value), jnp.sin(angle_value)], axis=1)


def parity_gram(received):
    sat_width = received.shape[-1]
    sat_block = received.reshape(received.shape[0], -1, sat_width)
    split_block = sat_block.reshape(sat_block.shape[0], sat_block.shape[1], 2, sat_width // 2)
    return jnp.einsum("irpa,irl->pial", split_block, sat_block, preferred_element_type=jnp.float32)


def shards(anomaly, row_weight, panel, order_value, deg_first, sat_rows, sat_slot):
    lat_count = lax.axis_size("lat")
    orb_count = lax.axis_size("orb")
    lat_index = lax.axis_index("lat")
    parity_index = lax.axis_index("ord")
    group_orders = panel.shape[1]
    row_count = panel.shape[2]
    half_count = panel.shape[4]
    lon_count = anomaly.shape[2]
    trig_table = fourier_table(order_value[0], lon_count)
    spectra = jnp.einsum(
        "hrk,kc->hrc", anomaly.astype(jnp.float32), trig_table, precision=lax.Precision.HIGHEST
    ) * math.sqrt(2.0 / lon_count)
    local_weight = lax.dynamic_slice_in_dim(row_weight, lat_index * row_count, row_count, 1)
    north_terms = spectra[0] * local_weight[0][:, None]
    south_terms = spectra[1] * local_weight[1][:, None]
    coefficients = jnp.stack(
        [
            north_terms[:, :group_orders],
            north_terms[:, group_orders:],
            south_terms[:, :group_orders],
            south_terms[:, group_orders:],
        ],
        axis=-1,
    )
    coefficients = jnp.transpose(coefficients, (1, 0, 2))[None].astype(jnp.bfloat16)
    own_order = lax.dynamic_slice_in_dim(order_value[0], lat_index, 1, 0)
    live_pair, sign_pair = window_flags(deg_first[0], own_order, half_count)
    live_own = lax.dynamic_index_in_dim(live_pair[0], parity_index, 0, keepdims=False)
    sign_own = lax.dynamic_index_in_dim(sign_pair[0], parity_index, 0, keepdims=False)
    live_mask = live_own.astype(jnp.bfloat16)
    panel_piece = panel[0, :, :, 0, :]
    coef_piece = coefficients[0]
    summed = lax.psum_scatter(
        jnp.einsum("ori,orc->oci", panel_piece, coef_piece, preferred_element_type=jnp.float32),
        "lat",
        scatter_dimension=0,
        tiled=True,
    )
    products = summed[0] * live_own[None, :]
    arrived_panel = lax.all_to_all(panel, "lat", split_axis=1, concat_axis=2, tiled=True)
    masked_own = arrived_panel[0, 0, :, 0, :] * live_mask[None, :]
    right_cos = products[0] + sign_own * products[2]
    right_sin = products[1] + sign_own * products[3]
    right_side = jnp.stack([right_cos, right_sin], axis=0)[None, None, :, None, :]
    parity_pair = lax.all_gather(masked_own[:, None, :], "ord", axis=1, tiled=True)
    plus_weight = (row_weight[0] + row_weight[1])[:, None, None]
    minus_weight = (row_weight[0] - row_weight[1])[:, None, None]
    plus_panel = (parity_pair.astype(jnp.float32) * plus_weight).astype(jnp.bfloat16)
    minus_panel = (parity_pair.astype(jnp.float32) * minus_weight).astype(jnp.bfloat16)
    full_plus = jnp.einsum(
        "ri,rqj->iqj", masked_own, plus_panel, preferred_element_type=jnp.float32
    )
    full_minus = jnp.einsum(
        "ri,rqj->iqj", masked_own, minus_panel, preferred_element_type=jnp.float32
    )
    same_parity = (jnp.arange(2, dtype=jnp.int32) == parity_index)[None, :, None]
    grid_normal = jnp.where(same_parity, full_plus, full_minus)
    sat_order = sat_slot[:, 0]
    sat_count = sat_order.shape[0]
    sat_width = sat_rows.shape[1]
    half_sat = sat_width // 2
    orders_all = orb_count * group_orders
    slot_cap = max(2, 2 * sat_count // orders_all)
    position = jnp.arange(sat_count, dtype=jnp.int32)
    earlier = (sat_order[:, None] == sat_order[None, :]) & (position[None, :] < position[:, None])
    slot_rank = jnp.sum(earlier, axis=1, dtype=jnp.int32)
    group_id = sat_order // group_orders
    within = sat_order % group_orders
    destination = (group_id * lat_count + within) * slot_cap + slot_rank
    reordered = (
        sat_rows.reshape(sat_count, half_sat, 2).transpose(0, 2, 1).reshape(sat_count, sat_width)
    )
    buffer = (
        jnp.zeros((orb_count * lat_count * slot_cap, sat_width), jnp.bfloat16)
        .at[destination]
        .set(reordered)
    )
    buffer = buffer.reshape(orb_count, lat_count, slot_cap, sat_width)
    arrived_rows = lax.all_to_all(
        lax.all_to_all(buffer, "lat", split_axis=1, concat_axis=1, tiled=True),
        "orb",
        split_axis=0,
        concat_axis=1,
        tiled=True,
    )
    own_gram = parity_gram(arrived_rows)
    sat_half = lax.psum_scatter(
        own_gram.reshape(-1, sat_width), "ord", scatter_dimension=0, tiled=True
    )
    sat_block = sat_half.reshape(half_sat, 2, half_sat)
    padded = jnp.pad(sat_block, ((0, half_count - half_sat), (0, 0), (0, half_count - half_sat)))
    normals = grid_normal + padded * (live_own[:, None, None] * live_pair[0][None, :, :])
    return (normals[None, None, None], right_side)


def solution(mesh):
    in_specs = (
        P(None, "lat", None),
        P(),
        P("orb", None, "lat", "ord", None),
        P("orb", None),
        P("orb", "lat"),
        P(("lat", "ord", "orb"), None),
        P(("lat", "ord", "orb"), None),
    )
    out_specs = (P("orb", "lat", "ord", None, None, None), P("orb", "lat", None, "ord", None))
    return jax.shard_map(shards, mesh=mesh, in_specs=in_specs, out_specs=out_specs, check_vma=False)
```

profile of v0, /device:TPU:1, one launch (start us, length us, event | category | flops | bytes accessed | tf_op | source)
XLA Modules:
  0.0 87.0 jit_solution(7779083475763705462)
XLA Ops:
  7.2 0.0 copy-start
  7.2 0.0 copy-start.3
  7.2 0.0 copy-start.2
  7.2 0.9 %convert_reduce_fusion = s32[256]{0:T(256)S(1)} fusion(s32[256]{0:T(256)} %bitcast.100), kind=kLoop, calls=%fused_computation.9 | loop fusion | flops 327424 | bytes 2048 | tf_op jit(solution)/shard_map/reduce_sum | solution.py:102
  8.1 0.7 compare_select_fusion.2
  8.8 1.0 %copy.60 = bf16[256,256]{0,1:T(8,128)(2,1)S(1)} copy(bf16[256,256]{1,0:T(8,128)(2,1)} %param.12) | data formatting | bytes 262144 | tf_op args[5]
  9.8 0.1 reshape.250
  9.9 0.1 copy.62
  10.0 1.5 %scatter_custom_fusion = bf16[512,256]{1,0:T(8,128)(2,1)S(1)} fusion(s32[256]{0:T(256)S(1)} %bitcast.102, bf16[256,256]{1,0:T(8,128)(2,1)S(1)} %copy.62, bf16[]{:T(256)} %constant.80.clone.1), kind=kCustom, calls=%fused_computation.18 | custom fusion | bytes 262146 | tf_op jit(solution)/shard_map/scatter | solution.py:112
  11.6 0.7 copy.63
  12.3 5.4 %all-to-all-start.1 = ((bf16[4,4,32,256]{3,2,0,1:T(8,128)(2,1)}), bf16[4,4,32,256]{3,2,0,1:T(8,128)(2,1)S(1)}, u32[]{:S(2)}, u32[]{:S(2)}) async-start(bf16[4,4,32,256]{3,2,0,1:T(8,128)(2,1)} %copy.63), calls=%async_computation.1 | async-start | bytes 524288 | tf_op jit(solution)/shard_map/all_to_all | solution.py:116
  18.4 0.8 constant_dynamic-slice_fusion.1
  19.2 1.2 %constant_dynamic-slice_fusion = s32[1,1]{1,0:T(1,128)} fusion(s32[1,4]{1,0:T(1,128)} %param.10, s32[]{:T(128)S(6)} %select_n.60), kind=kLoop, calls=%fused_computation.79 | loop fusion | bytes 12 | tf_op jit(solution)/shard_map/dynamic_slice | solution.py:62
  20.4 1.3 %fusion.23 = (f32[4320,4]{0,1:T(4,128)S(1)}, f32[4320,4]{0,1:T(4,128)S(1)}) fusion(s32[4]{0:T(128)} %bitcast.103), kind=kLoop, calls=%fused_computation.34 | loop fusion | flops 155520 | bytes 138256 | tf_op jit(solution)/shard_map/cos | solution.py:26
  21.7 0.0 copy-done
  21.7 1.0 %fusion = f32[2,16,8]{1,2,0:T(8,128)S(1)} fusion(bf16[2,16,4320]{2,1,0:T(8,128)(2,1)S(1)} %copy-done, f32[4320,4]{0,1:T(4,128)S(1)} %get-tuple-element.27, f32[4320,4]{0,1:T(4,128)S(1)} %get-tuple-element.26), kind=kOutput, calls=%fused_computation.4 | convolution fusion | flops 13305856 | bytes 415744 | tf_op jit(solution)/shard_map/hrk,kc->hrc/dot_general | solution.py:46
  22.7 0.1 fusion.29
  22.9 1.0 %fusion.13 = f32[4,4,640]{2,1,0:T(4,128)S(1)} fusion(bf16[1,4,16,1,640]{4,2,3,1,0:T(8,128)(2,1)} %param.9, bf16[16,4,1]{0,2,1:T(2,128)(2,1)S(1)} %copy.71, bf16[16,4,1]{0,2,1:T(2,128)(2,1)S(1)} %copy.70, bf16[16,4,1]{0,2,1:T(2,128)(2,1)S(1)} %copy.69, bf16[16,4,1]{0,2,1:T(2,128)(2,1)S(1)} %copy.68), kind=kOutput, calls=%fused_computation.21 | convolution fusion | flops 329728 | bytes 123392 | tf_op jit(solution)/shard_map/ori,orc->oci/dot_general | solution.py:70
  23.9 15.8 %all-reduce.1 = f32[4,4,640]{2,1,0:T(4,128)S(1)} all-reduce(f32[4,4,640]{2,1,0:T(4,128)S(1)} %fusion.13), channel_id=3, replica_groups=mesh['lat'=4,'ord'=2,'orb'=4] {'lat'}, use_global_device_ids=true, to_apply=%region_3.4.clone | all-reduce | flops 10240 | bytes 81920
  39.7 0.0 copy-done.3
  39.8 0.7 dynamic-slice.3
  40.4 0.6 compare_convert_fusion
  41.0 0.7 compare_select_fusion
  41.7 0.0 copy-start.1
  41.7 0.7 fusion.24
  42.4 0.0 copy-done.2
  42.4 0.6 subtract_bitcast_fusion
  43.1 0.0 all-to-all-done.1
  43.1 3.3 %all-to-all-start = ((bf16[1,4,16,1,640]{4,2,3,0,1:T(8,128)(2,1)}), bf16[1,4,16,1,640]{4,2,3,0,1:T(8,128)(2,1)S(1)}, u32[]{:S(2)}, u32[]{:S(2)}) async-start(bf16[1,4,16,1,640]{4,2,3,0,1:T(8,128)(2,1)} %bitcast), calls=%async_computation | async-start | bytes 163840 | tf_op jit(solution)/shard_map/all_to_all | solution.py:76
  46.4 0.6 copy.73
  47.0 0.5 iota_compare_fusion.1
  47.5 0.7 copy.64
  48.2 2.7 %all-to-all-done = bf16[1,4,16,1,640]{4,2,3,0,1:T(8,128)(2,1)S(1)} async-done(((bf16[1,4,16,1,640]{4,2,3,0,1:T(8,128)(2,1)}), bf16[1,4,16,1,640]{4,2,3,0,1:T(8,128)(2,1)S(1)}, u32[]{:S(2)}, u32[]{:S(2)}) %all-to-all-start) | async-done | bytes 81952 | tf_op jit(solution)/shard_map/all_to_all | solution.py:76
  51.0 3.4 %all-to-all-start.2 = ((bf16[4,4,32,256]{3,2,1,0:T(8,128)(2,1)}), bf16[4,4,32,256]{3,2,1,0:T(8,128)(2,1)S(1)}, u32[]{:S(2)}, u32[]{:S(2)}) async-start(bf16[4,4,32,256]{3,2,1,0:T(8,128)(2,1)} %copy.64), calls=%async_computation.2 | async-start | bytes 524288 | tf_op jit(solution)/shard_map/all_to_all | solution.py:115
  54.4 0.0 reduce-scatter.2.cloned.1.call-start
  54.5 8.1 %all_gather.3 = bf16[64,2,640]{2,0,1:T(8,128)(2,1)} all-gather(bf16[64,1,640]{2,0,1:T(8,128)(2,1)S(1)} %broadcast_multiply_fusion), channel_id=1, replica_groups=mesh['lat'=4,'ord'=2,'orb'=4] {'ord'}, dimensions={1}, use_global_device_ids=true | all-gather | bytes 245760 | tf_op jit(solution)/shard_map/all_gather | solution.py:81
  62.6 0.0 all-to-all-done.2
  62.6 0.1 reshape.254
  62.6 0.2 copy.65
  62.8 0.2 convolution_bitcast_fusion
  63.0 0.8 copy.66
  63.9 0.0 reduce-scatter.2.cloned.1.call-update
  63.9 0.6 bitcast_multiply_fusion
  64.6 1.6 %fusion.5 = f32[640,2,640]{2,0,1:T(8,128)S(1)} fusion(bf16[64,2,640]{2,0,1:T(8,128)(2,1)} %all_gather.3, f32[64]{0:T(128)} %get-tuple-element.25, bf16[64,640]{1,0:T(8,128)(2,1)} %bitcast_multiply_fusion), kind=kOutput, calls=%fused_computation.12 | convolution fusion | flops 105103360 | bytes 3522816 | tf_op jit(solution)/shard_map/ri,rqj->iqj/dot_general | solution.py:86
  66.2 6.4 %reduce-scatter.2.cloned.1.call-done = f32[128,256]{0,1:T(8,128)} async-done(((f32[256,256]{0,1:T(8,128)}), f32[128,256]{0,1:T(8,128)}) %reduce-scatter.2.cloned.1.call-update) | async-done | bytes 131088 | tf_op jit(solution)/shard_map/reduce_scatter | solution.py:123
  72.5 1.7 %copy.67 = f32[128,2,128]{2,0,1:T(8,128)} copy(f32[128,2,128]{0,2,1:T(8,128)} %bitcast.99) | data formatting | bytes 262144 | tf_op jit(solution)/shard_map/reshape | solution.py:126
  74.2 1.7 %add_bitcast_fusion = f32[1,1,1,640,2,640]{5,3,4,2,1,0:T(8,128)S(1)} fusion(f32[128,2,128]{2,0,1:T(8,128)} %copy.67, f32[640,2,640]{2,0,1:T(8,128)S(1)} %fusion.5, f32[2,640]{1,0:T(2,128)} %compare_convert_fusion, f32[640]{0:T(1024)} %copy-done.1, pred[2]{0:T(512)(128)(4,1)} %iota_compare_fusion.1, bf16[64,2,640]{2,0,1:T(8,128)(2,1)} %all_gather.3, ...), kind=kOutput, calls=%fused_computation.1 | convolution fusion | flops 108380160 | bytes 6938370 | tf_op jit(solution)/shard_map/ri,rqj->iqj/dot_general | solution.py:89
  75.9 4.2 %copy.72 = f32[1,1,1,640,2,640]{5,4,3,2,1,0:T(2,128)} copy(f32[1,1,1,640,2,640]{5,3,4,2,1,0:T(8,128)S(1)} %add_bitcast_fusion) | data formatting | bytes 6553600
  (14 shorter events, 0.1 us)
Async XLA Ops:
  7.2 14.5 %copy-start = (bf16[2,16,4320]{2,1,0:T(8,128)(2,1)S(1)}, bf16[2,16,4320]{2,1,0:T(8,128)(2,1)}, u32[]{:S(2)}) copy-start(bf16[2,16,4320]{2,1,0:T(8,128)(2,1)} %param.7) | copy-start | bytes 829444
  7.2 32.6 %copy-start.3 = (u32[32]{0:T(128)S(1)}, u32[32]{0:T(128)}, u32[]{:S(2)}) copy-start(u32[32]{0:T(128)} %constant.103) | copy-start | bytes 388
  7.2 35.2 %copy-start.2 = (f32[2,64]{1,0:T(2,128)S(1)}, f32[2,64]{1,0:T(2,128)}, u32[]{:S(2)}) copy-start(f32[2,64]{1,0:T(2,128)} %param.8) | copy-start | bytes 1540
  12.3 30.7 %all-to-all-start.1 = ((bf16[4,4,32,256]{3,2,0,1:T(8,128)(2,1)}), bf16[4,4,32,256]{3,2,0,1:T(8,128)(2,1)S(1)}, u32[]{:S(2)}, u32[]{:S(2)}) async-start(bf16[4,4,32,256]{3,2,0,1:T(8,128)(2,1)} %copy.63), calls=%async_computation.1 | async-start | bytes 524288 | tf_op jit(solution)/shard_map/all_to_all | solution.py:116
  41.7 12.7 %copy-start.1 = (f32[640]{0:T(1024)}, f32[640]{0:T(1024)S(1)}, u32[]{:S(2)}) copy-start(f32[640]{0:T(1024)S(1)} %fusion.36) | copy-start | bytes 7684
  43.1 7.9 %all-to-all-start = ((bf16[1,4,16,1,640]{4,2,3,0,1:T(8,128)(2,1)}), bf16[1,4,16,1,640]{4,2,3,0,1:T(8,128)(2,1)S(1)}, u32[]{:S(2)}, u32[]{:S(2)}) async-start(bf16[1,4,16,1,640]{4,2,3,0,1:T(8,128)(2,1)} %bitcast), calls=%async_computation | async-start | bytes 163840 | tf_op jit(solution)/shard_map/all_to_all | solution.py:76
  51.0 11.6 %all-to-all-start.2 = ((bf16[4,4,32,256]{3,2,1,0:T(8,128)(2,1)}), bf16[4,4,32,256]{3,2,1,0:T(8,128)(2,1)S(1)}, u32[]{:S(2)}, u32[]{:S(2)}) async-start(bf16[4,4,32,256]{3,2,1,0:T(8,128)(2,1)} %copy.64), calls=%async_computation.2 | async-start | bytes 524288 | tf_op jit(solution)/shard_map/all_to_all | solution.py:115
  54.4 18.1 %reduce-scatter.2.cloned.1.call-start = ((), (), s32[]{:S(2)}) async-start(), calls=%async_computation.4 | async-start | bytes 393216 | tf_op jit(solution)/shard_map/reduce_scatter | solution.py:123
Sparse Core Ops, SparseCore 0:
  64.0 8.4 reduce-scatter.1
where the time goes:
time: 87.8 us; the launch traced here: 87 us
  blocking collectives  23.9 us (27%)
  between operations  14.9 us (17%)
  local copies, waits for them, and re-layouts  14.4 us (16%)
  starting transfers between devices  12.2 us (14%)
  waiting for transfers between devices  9.13 us (10%)
  other arithmetic  6.78 us (8%)
  matrix products  5.57 us (6%)
    unnamed x1, blocking collectives  15.8 us
    all_gather x1, blocking collectives, shards(): lax.all_gather(masked_own[:, None, :], 'ord', axis=1, tiled=True)  8.09 us
    unnamed x12, local copies, waits for them, and re-layouts  6.53 us
    reduce_scatter x1, waiting for transfers between devices, shards(): lax.psum_scatter(own_gram.reshape(-1, sat_width), 'ord', scatter_dimensio...  6.36 us
    all_to_all x1, starting transfers between devices, shards(): lax.all_to_all(buffer, 'lat', split_axis=1, concat_axis=1, tiled=True)  5.42 us
    all_to_all x1, starting transfers between devices, shards(): lax.all_to_all(lax.all_to_all(buffer, 'lat', split_axis=1, concat_axis=1,...  3.44 us
    all_to_all x1, starting transfers between devices, shards(): lax.all_to_all(panel, 'lat', split_axis=1, concat_axis=2, tiled=True)  3.31 us
    all_to_all x1, waiting for transfers between devices, shards(): lax.all_to_all(panel, 'lat', split_axis=1, concat_axis=2, tiled=True)  2.75 us
  transfers between devices with their start and end apart: 4, of which 2 were waited for; matrix products, arithmetic and copies ran while one was open for 15% of the time, Pallas kernels for 0%

commit v1 on v0

v1 whole, which is shorter than its diff:
```python
import functools
import math

import jax
import jax.numpy as jnp
from jax import lax
from jax.experimental import pallas as pl
from jax.experimental.pallas import tpu as pltpu
from jax.experimental.layout import Layout, with_layout_constraint
from jax.sharding import PartitionSpec as P

LMAX = 2190
MESH = pl.DeviceIdType.MESH
F32 = jnp.float32
BF16 = jnp.bfloat16
LANES = 128


def iota(shape, dim):
    return lax.broadcasted_iota(jnp.int32, shape, dim)


def dot_tn(a, b):
    return lax.dot_general(a, b, (((0,), (0,)), ((), ())), preferred_element_type=F32)


def dot_nt(a, b):
    return lax.dot_general(a, b, (((1,), (1,)), ((), ())), preferred_element_type=F32)


def dot_nn(a, b):
    return jnp.dot(a, b, preferred_element_type=F32)


def exchange_kernel(
    sizes,
    anomaly, weight, panel, order, sat_rows, slot_row,
    panels, coefs, sat_out,
    bucket, arrived, coef_mine, gram_send, gram_recv,
    panel_s, panel_r, coef_s, coef_r, sat_s, sat_r, pair_s, pair_r,
):
    n_lat, n_orb = sizes
    group_orders, row_count, half_count = panel.shape
    sat_count, width = sat_rows.shape
    half = width // 2
    cap = bucket.shape[1]
    slots = bucket.shape[0]
    n_src = n_lat * n_orb
    lon = anomaly.shape[2]
    lat = lax.axis_index("lat")
    par = lax.axis_index("ord")
    orb = lax.axis_index("orb")
    other = 1 - par
    me = lat * n_orb + orb

    def peer(k):
        p = lax.rem(me + k, n_src)
        return p, p // n_orb, lax.rem(p, n_orb)

    barrier = pltpu.get_barrier_semaphore()
    pl.semaphore_signal(barrier, inc=1, device_id=(lat, other, orb), device_id_type=MESH)

    def greet(k, c):
        _, a, b = peer(k)
        pl.semaphore_signal(barrier, inc=1, device_id=(a, par, b), device_id_type=MESH)
        return c

    lax.fori_loop(1, n_src, greet, 0)

    perm = (iota((width, width), 0)
            == 2 * (iota((width, width), 1) % half) + iota((width, width), 1) // half)
    split_rows = dot_nn(sat_rows[...], perm.astype(F32).astype(BF16)).astype(BF16)
    row = slot_row[...].astype(F32)
    sub = iota((sat_count, sat_count), 0)
    lane = iota((sat_count, sat_count), 1)
    column = jnp.sum(jnp.where(sub == lane, row, 0.0), axis=1, keepdims=True)
    earlier = (column == row) & (sub < lane)
    rank = jnp.sum(jnp.where(earlier, 1.0, 0.0), axis=0, keepdims=True)
    target = row * float(cap) + rank
    step_slots = max(1, min(slots, 512 // cap))

    def fill(i, c):
        spot = (iota((step_slots * cap, sat_count), 0) + i * (step_slots * cap)).astype(F32)
        hot = jnp.where(spot == target, 1.0, 0.0).astype(BF16)
        rows = dot_nn(hot, split_rows).astype(BF16)
        bucket[pl.ds(i * step_slots, step_slots)] = rows.reshape(step_slots, cap, width)
        return c

    if slots == step_slots:
        fill(0, 0)
    else:
        lax.fori_loop(0, slots // step_slots, fill, 0)

    pl.semaphore_wait(barrier, n_src)

    def panel_copy(dst, src):
        return pltpu.make_async_remote_copy(
            src_ref=panel.at[dst], dst_ref=panels.at[par, src],
            send_sem=panel_s.at[dst], recv_sem=panel_r.at[src],
            device_id=(dst, par, orb), device_id_type=MESH)

    def sat_copy(dst, a, b, src):
        return pltpu.make_async_remote_copy(
            src_ref=bucket.at[b * group_orders + a], dst_ref=arrived.at[src],
            send_sem=sat_s.at[dst], recv_sem=sat_r.at[src],
            device_id=(a, par, b), device_id_type=MESH)

    def coef_copy(dst, src):
        return pltpu.make_async_remote_copy(
            src_ref=coef_mine, dst_ref=coefs.at[src],
            send_sem=coef_s.at[dst], recv_sem=coef_r.at[src],
            device_id=(dst, par, orb), device_id_type=MESH)

    def forward():
        return pltpu.make_async_remote_copy(
            src_ref=panels.at[par], dst_ref=panels.at[par],
            send_sem=pair_s.at[0], recv_sem=pair_r.at[0],
            device_id=(lat, other, orb), device_id_type=MESH)

    def backward():
        return pltpu.make_async_remote_copy(
            src_ref=panels.at[par], dst_ref=panels.at[other],
            send_sem=pair_s.at[0], recv_sem=pair_r.at[0],
            device_id=(lat, other, orb), device_id_type=MESH)

    def gram_copy():
        return pltpu.make_async_remote_copy(
            src_ref=gram_send, dst_ref=gram_recv,
            send_sem=pair_s.at[1], recv_sem=pair_r.at[1],
            device_id=(lat, other, orb), device_id_type=MESH)

    def each_lat(action):
        def body(k, c):
            action(lax.rem(lat + k, n_lat))
            return c

        lax.fori_loop(1, n_lat, body, 0)

    def each_src(action):
        def body(k, c):
            action(*peer(k))
            return c

        lax.fori_loop(1, n_src, body, 0)

    each_lat(lambda dst: panel_copy(dst, lat).start())
    each_src(lambda p, a, b: sat_copy(p, a, b, me).start())
    arrived[me] = bucket[orb * group_orders + lat]
    panels[par, lat] = panel[lat]

    wide = 2 * group_orders
    line = iota((wide, group_orders), 0)
    pick = lax.rem(line, group_orders) == iota((wide, group_orders), 1)
    order_col = jnp.sum(
        jnp.where(pick, order[...].astype(F32), 0.0), axis=1, keepdims=True)
    sample = iota((wide, lon), 1).astype(F32)
    x = sample * order_col
    r = x - jnp.floor(x * (1.0 / lon)) * float(lon)
    r = r - jnp.where(iota((wide, lon), 0) >= group_orders, lon / 4.0, 0.0)
    r = r - jnp.floor(r * (1.0 / lon) + 0.5) * float(lon)
    z = (lon / 4.0 - jnp.abs(r)) * (2.0 * math.pi / lon)
    z2 = z * z
    poly = -1.0 / math.factorial(11)
    for d in (9, 7, 5, 3, 1):
        sgn = 1.0 if d % 4 == 1 else -1.0
        poly = poly * z2 + sgn / math.factorial(d)
    trig = poly * z
    high = trig.astype(BF16)
    low = (trig - high.astype(F32)).astype(BF16)
    coef_mine[...] = jnp.zeros_like(coef_mine)
    total_rows = weight.shape[1]
    here = (iota((row_count, total_rows), 1)
            == iota((row_count, total_rows), 0) + lat * row_count)
    scale = math.sqrt(2.0 / lon)
    for h in range(2):
        data = anomaly[h]
        spectrum = (dot_nt(data, high) + dot_nt(data, low)) * scale
        own_weight = jnp.sum(
            jnp.where(here, weight[h:h + 1, :], 0.0), axis=1, keepdims=True)
        coef_mine[h, :, 0:wide] = (spectrum * own_weight).astype(BF16)
    each_lat(lambda dst: coef_copy(dst, lat).start())
    coefs[lat] = coef_mine[...]

    each_lat(lambda src: panel_copy(src, src).wait_recv())
    forward().start()
    each_src(lambda p, a, b: sat_copy(p, a, b, p).wait_recv())

    chunk = max(1, min(n_src, 512 // cap))
    steps = n_src // chunk

    def gram(which):
        cols = pl.ds(pl.multiple_of(which * half, half), half)

        def part(i):
            full = arrived[pl.ds(i * chunk, chunk)].reshape(chunk * cap, width)
            some = arrived[pl.ds(i * chunk, chunk), :, cols].reshape(chunk * cap, half)
            return dot_tn(some, full)

        if steps == 1:
            return part(0)
        return lax.fori_loop(
            0, steps, lambda i, c: c + part(i), jnp.zeros((half, width), F32))

    gram_send[...] = gram(other)
    gram_copy().start()
    own = gram(par)
    each_lat(lambda src: coef_copy(src, src).wait_recv())
    backward().wait_recv()
    gram_copy().wait_recv()
    sat_out[...] = own + gram_recv[...]
    each_lat(lambda dst: panel_copy(dst, lat).wait_send())
    each_lat(lambda dst: coef_copy(dst, lat).wait_send())
    each_src(lambda p, a, b: sat_copy(p, a, b, me).wait_send())
    forward().wait_send()
    gram_copy().wait_send()


def normal_kernel(order, first, weight, panels, coefs, sat, out, right, left, sides):
    step = pl.program_id(0)
    lat = lax.axis_index("lat")
    par = lax.axis_index("ord")
    _, n_lat, row_count, half_count = panels.shape
    total = n_lat * row_count
    tile, width = sat.shape
    stripes = half_count // LANES
    base = first[0, 0]
    group_orders = order.shape[1]
    limit = LMAX - base

    @pl.when(step == 0)
    def _():
        for l in range(n_lat):
            rows = slice(l * row_count, (l + 1) * row_count)
            here = (iota((row_count, total), 1) == iota((row_count, total), 0) + l * row_count)
            north = jnp.sum(jnp.where(here, weight[0:1, :], 0.0), axis=1, keepdims=True)
            south = jnp.sum(jnp.where(here, weight[1:2, :], 0.0), axis=1, keepdims=True)
            for q in range(2):
                live = 2 * iota((row_count, half_count), 1) + q <= limit
                masked = jnp.where(live, panels[q, l].astype(F32), 0.0)
                factor = jnp.where(par == q, north + south, north - south)
                sides[q, rows, :] = (masked * factor).astype(BF16)
            live = 2 * iota((row_count, half_count), 1) + par <= limit
            left[rows, :] = jnp.where(live, panels[par, l].astype(F32), 0.0).astype(BF16)
        sign = 1.0 - 2.0 * lax.rem(base + par + order[0, lat], 2).astype(F32)
        masked = left[...]
        north = dot_tn(coefs[:, 0].reshape(total, LANES), masked)
        south = dot_tn(coefs[:, 1].reshape(total, LANES), masked)
        both = north + sign * south
        place = iota((LANES, half_count), 0)
        for t in range(2):
            right[t] = jnp.sum(
                jnp.where(place == t * group_orders + lat, both, 0.0), axis=0, keepdims=True)

    cols = pl.ds(pl.multiple_of(step * tile, tile), tile)
    block = left[:, cols]
    for q in range(2):
        value = dot_tn(block, sides[q])
        for b in range(stripes):
            out[pl.ds(2 * b + q, tile, stride=2 * stripes), :] = (
                value[:, b * LANES:(b + 1) * LANES])

    @pl.when(step == 0)
    def _():
        half = width // 2
        for q in range(2):
            for b in range(half // LANES):
                at = pl.ds(2 * b + q, tile, stride=2 * stripes)
                keep = ((2 * iota((tile, LANES), 0) + par <= limit)
                        & (2 * (iota((tile, LANES), 1) + b * LANES) + q <= limit))
                piece = sat[:, q * half + b * LANES:q * half + (b + 1) * LANES]
                out[at, :] = out[at, :] + jnp.where(keep, piece, 0.0)


def shards(sizes, anomaly, row_weight, panel, order_value, deg_first, sat_rows, sat_slot):
    n_lat, n_orb = sizes
    _, group_orders, row_count, _, half_count = panel.shape
    sat_count, width = sat_rows.shape
    half = width // 2
    total = n_lat * row_count
    slots = n_orb * group_orders
    n_src = n_lat * n_orb
    cap = max(16, 2 * sat_count // slots)
    vmem = pl.BlockSpec(memory_space=pltpu.VMEM)
    smem = pl.BlockSpec(memory_space=pltpu.SMEM)
    dma = pltpu.SemaphoreType.DMA
    panels, coefs, sat = pl.pallas_call(
        functools.partial(exchange_kernel, sizes),
        out_shape=(
            jax.ShapeDtypeStruct((2, n_lat, row_count, half_count), BF16),
            jax.ShapeDtypeStruct((n_lat, 2, row_count, LANES), BF16),
            jax.ShapeDtypeStruct((half, width), F32),
        ),
        in_specs=[vmem] * 6,
        out_specs=[vmem] * 3,
        scratch_shapes=[
            pltpu.VMEM((slots, cap, width), BF16),
            pltpu.VMEM((n_src, cap, width), BF16),
            pltpu.VMEM((2, row_count, LANES), BF16),
            pltpu.VMEM((half, width), F32),
            pltpu.VMEM((half, width), F32),
            dma((n_lat,)), dma((n_lat,)), dma((n_lat,)), dma((n_lat,)),
            dma((n_src,)), dma((n_src,)), dma((2,)), dma((2,)),
        ],
        compiler_params=pltpu.CompilerParams(
            collective_id=0, has_side_effects=True, vmem_limit_bytes=40 * 2**20),
        name="exchange",
    )(
        anomaly,
        row_weight,
        panel.reshape(group_orders, row_count, half_count),
        order_value,
        sat_rows,
        sat_slot.reshape(1, sat_count),
    )
    stripes = half_count // LANES
    flat, right = pl.pallas_call(
        normal_kernel,
        grid=(half_count // half,),
        out_shape=(
            jax.ShapeDtypeStruct((half_count * 2 * stripes, LANES), F32),
            jax.ShapeDtypeStruct((2, 1, half_count), F32),
        ),
        in_specs=[smem, smem, vmem, vmem, vmem, vmem],
        out_specs=[
            pl.BlockSpec((half * 2 * stripes, LANES), lambda i: (i, 0)),
            pl.BlockSpec((2, 1, half_count), lambda i: (0, 0, 0)),
        ],
        scratch_shapes=[
            pltpu.VMEM((total, half_count), BF16),
            pltpu.VMEM((2, total, half_count), BF16),
        ],
        compiler_params=pltpu.CompilerParams(
            dimension_semantics=("arbitrary",), vmem_limit_bytes=40 * 2**20),
        name="normal",
    )(order_value, deg_first, row_weight, panels, coefs, sat)
    normals = flat.reshape(half_count, stripes, 2, LANES).transpose(0, 2, 1, 3)
    normals = with_layout_constraint(normals, Layout((0, 2, 1, 3)))
    normals = normals.reshape(1, 1, 1, half_count, 2, half_count)
    return normals, right.reshape(1, 1, 2, 1, half_count)


def solution(mesh):
    sizes = (mesh.shape["lat"], mesh.shape["orb"])
    in_specs = (
        P(None, "lat", None),
        P(),
        P("orb", None, "lat", "ord", None),
        P("orb", None),
        P("orb", "lat"),
        P(("lat", "ord", "orb"), None),
        P(("lat", "ord", "orb"), None),
    )
    out_specs = (P("orb", "lat", "ord", None, None, None), P("orb", "lat", None, "ord", None))
    return jax.shard_map(
        functools.partial(shards, sizes), mesh=mesh, in_specs=in_specs,
        out_specs=out_specs, check_vma=False)
```

time: 87.8 us -> 27.4 us (0.31)
  the two profiles are of different devices: /device:TPU:1 before, /device:TPU:0 now
where the time goes in v1:
time: 27.4 us; the launch traced here: 27.1 us
  Pallas kernels  21.1 us (77%)
  local copies, waits for them, and re-layouts  4.75 us (17%)
  between operations  1.3 us (5%)
    pallas_call x1, Pallas kernels, shards(): pl.pallas_call(functools.partial(exchange_kernel, sizes), out_shape=(jax....  16.8 us
    unnamed x12, local copies, waits for them, and re-layouts  4.75 us
    pallas_call x1, Pallas kernels, shards(): pl.pallas_call(normal_kernel, grid=(half_count // half,), out_shape=(jax....  4.29 us

profile of v1, /device:TPU:0, one launch (start us, length us, event | category | flops | bytes accessed | tf_op | source)
XLA Modules:
  0.0 27.1 jit_solution(1275011230423692189)
XLA Ops:
  1.3 0.0 copy-start
  1.3 0.9 %copy-done = bf16[2,16,4320]{2,1,0:T(8,128)(2,1)S(1)} copy-done((bf16[2,16,4320]{2,1,0:T(8,128)(2,1)S(1)}, bf16[2,16,4320]{2,1,0:T(8,128)(2,1)}, u32[]{:S(2)}) %copy-start) | copy-done | bytes 276504
  2.2 0.0 copy-start.1
  2.2 0.9 %copy-done.1 = bf16[256,256]{1,0:T(8,128)(2,1)S(1)} copy-done((bf16[256,256]{1,0:T(8,128)(2,1)S(1)}, bf16[256,256]{1,0:T(8,128)(2,1)}, u32[]{:S(2)}) %copy-start.1) | copy-done | bytes 131096
  3.1 0.0 copy-start.2
  3.1 0.9 %copy-done.2 = bf16[1,4,16,1,640]{4,2,3,1,0:T(8,128)(2,1)S(1)} copy-done((bf16[1,4,16,1,640]{4,2,3,1,0:T(8,128)(2,1)S(1)}, bf16[1,4,16,1,640]{4,2,3,1,0:T(8,128)(2,1)}, u32[]{:S(2)}) %copy-start.2) | copy-done | bytes 81944
  4.0 0.0 copy-start.3
  4.0 0.7 %copy-done.3 = f32[2,64]{1,0:T(2,128)S(1)} copy-done((f32[2,64]{1,0:T(2,128)S(1)}, f32[2,64]{1,0:T(2,128)}, u32[]{:S(2)}) %copy-start.3) | copy-done | bytes 536
  4.7 0.0 copy-start.4
  4.7 0.7 %copy-done.4 = s32[1,4]{1,0:T(1,128)S(1)} copy-done((s32[1,4]{1,0:T(1,128)S(1)}, s32[1,4]{1,0:T(1,128)}, u32[]{:S(2)}) %copy-start.4) | copy-done | bytes 40
  5.4 0.0 copy-start.5
  5.4 0.7 %copy-done.5 = s32[256,1]{0,1:T(1,128)S(1)} copy-done((s32[256,1]{0,1:T(1,128)S(1)}, s32[256,1]{0,1:T(1,128)}, u32[]{:S(2)}) %copy-start.5) | copy-done | bytes 1048
  6.0 16.8 %exchange.1 = (bf16[2,4,16,640]{3,2,1,0:T(8,128)(2,1)S(1)}, bf16[4,2,16,128]{3,2,1,0:T(8,128)(2,1)S(1)}, f32[128,256]{1,0:T(8,128)S(1)}) custom-call(bf16[2,16,4320]{2,1,0:T(8,128)(2,1)S(1)} %copy-done, f32[2,64]{1,0:T(2,128)S(1)} %copy-done.3, bf16[4,16,640]{2,1,0:T(8,128)(2,1)S(1)} %bitcast.8, s32[1,4]{1,0:T(1,128)S(1)} %copy-done.4, ...), custom_call_target="tpu_custom_call" | custom-call | tf_op jit(solution)/shard_map/exchange/pallas_call | solution.py:286
  22.8 4.3 %normal.1 = (f32[6400,128]{1,0:T(8,128)}, f32[2,1,640]{2,1,0:T(1,128)}) custom-call(s32[1,4]{1,0:T(1,128)S(1)} %copy-done.4, s32[1,1]{1,0:T(1,128)S(6)} %copy.9.first, f32[2,64]{1,0:T(2,128)S(1)} %copy-done.3, bf16[2,4,16,640]{3,2,1,0:T(8,128)(2,1)S(1)} %get-tuple-element.7.panels, bf16[4,2,16,128]{3,2,1,0:T(8,128)(2,1)S(1)} %get-tuple-element.8.coefs, ...), custom_call_target="tpu_custom_call" | custom-call | tf_op jit(solution)/shard_map/normal/pallas_call | solution.py:316
Async XLA Ops:
  1.3 1.0 %copy-start = (bf16[2,16,4320]{2,1,0:T(8,128)(2,1)S(1)}, bf16[2,16,4320]{2,1,0:T(8,128)(2,1)}, u32[]{:S(2)}) copy-start(bf16[2,16,4320]{2,1,0:T(8,128)(2,1)} %anomaly.1) | copy-start | bytes 829444
  2.2 0.9 %copy-start.1 = (bf16[256,256]{1,0:T(8,128)(2,1)S(1)}, bf16[256,256]{1,0:T(8,128)(2,1)}, u32[]{:S(2)}) copy-start(bf16[256,256]{1,0:T(8,128)(2,1)} %sat_rows.1) | copy-start | bytes 393220
  3.1 0.9 %copy-start.2 = (bf16[1,4,16,1,640]{4,2,3,1,0:T(8,128)(2,1)S(1)}, bf16[1,4,16,1,640]{4,2,3,1,0:T(8,128)(2,1)}, u32[]{:S(2)}) copy-start(bf16[1,4,16,1,640]{4,2,3,1,0:T(8,128)(2,1)} %param.9) | copy-start | bytes 245764
  4.0 0.7 %copy-start.3 = (f32[2,64]{1,0:T(2,128)S(1)}, f32[2,64]{1,0:T(2,128)}, u32[]{:S(2)}) copy-start(f32[2,64]{1,0:T(2,128)} %weight.3) | copy-start | bytes 1540
  4.7 0.7 %copy-start.4 = (s32[1,4]{1,0:T(1,128)S(1)}, s32[1,4]{1,0:T(1,128)}, u32[]{:S(2)}) copy-start(s32[1,4]{1,0:T(1,128)} %order.3) | copy-start | bytes 52
  5.4 0.7 %copy-start.5 = (s32[256,1]{0,1:T(1,128)S(1)}, s32[256,1]{0,1:T(1,128)}, u32[]{:S(2)}) copy-start(s32[256,1]{0,1:T(1,128)} %param.13) | copy-start | bytes 3076

commit v2 on v1

v2 whole, which is shorter than its diff:
```python
import functools
import math

import jax
import jax.numpy as jnp
from jax import lax
from jax.experimental import pallas as pl
from jax.experimental.pallas import tpu as pltpu
from jax.experimental.layout import Layout, with_layout_constraint
from jax.sharding import PartitionSpec as P

LMAX = 2190
MESH = pl.DeviceIdType.MESH
F32 = jnp.float32
BF16 = jnp.bfloat16
LANES = 128


def iota(shape, dim):
    return lax.broadcasted_iota(jnp.int32, shape, dim)


def dot_tn(a, b):
    return lax.dot_general(a, b, (((0,), (0,)), ((), ())), preferred_element_type=F32)


def dot_nt(a, b):
    return lax.dot_general(a, b, (((1,), (1,)), ((), ())), preferred_element_type=F32)


def dot_nn(a, b):
    return jnp.dot(a, b, preferred_element_type=F32)


def exchange_kernel(
    sizes,
    order, first, anomaly_hbm, weight_hbm, panel, sat_hbm, slot_hbm,
    out_hbm, right_hbm,
    out, right, anomaly, weight, sat_rows, slot_row, panels, coefs,
    bucket, arrived, coef_mine, gram_send, gram_recv, left, sides,
    load, save, panel_s, panel_r, coef_s, coef_r, sat_s, sat_r, pair_s, pair_r,
):
    n_lat, n_orb = sizes
    group_orders, row_count, half_count = panel.shape
    sat_count, width = sat_rows.shape
    half = width // 2
    cap = bucket.shape[1]
    slots = bucket.shape[0]
    n_src = n_lat * n_orb
    lon = anomaly.shape[2]
    lat = lax.axis_index("lat")
    par = lax.axis_index("ord")
    orb = lax.axis_index("orb")
    other = 1 - par
    stripes = half_count // LANES
    base = first[0, 0]
    limit = LMAX - base
    me = lat * n_orb + orb

    def peer(k):
        p = lax.rem(me + k, n_src)
        return p, p // n_orb, lax.rem(p, n_orb)

    loads = [
        pltpu.make_async_copy(sat_hbm, sat_rows, load.at[0]),
        pltpu.make_async_copy(slot_hbm, slot_row, load.at[1]),
        pltpu.make_async_copy(anomaly_hbm, anomaly, load.at[2]),
        pltpu.make_async_copy(weight_hbm, weight, load.at[3]),
        pltpu.make_async_copy(panel.at[lat], panels.at[par, lat], load.at[4]),
    ]
    for one in loads:
        one.start()
    barrier = pltpu.get_barrier_semaphore()
    pl.semaphore_signal(barrier, inc=1, device_id=(lat, other, orb), device_id_type=MESH)

    def greet(k, c):
        _, a, b = peer(k)
        pl.semaphore_signal(barrier, inc=1, device_id=(a, par, b), device_id_type=MESH)
        return c

    lax.fori_loop(1, n_src, greet, 0)

    def panel_copy(dst, src):
        return pltpu.make_async_remote_copy(
            src_ref=panel.at[dst], dst_ref=panels.at[par, src],
            send_sem=panel_s.at[dst], recv_sem=panel_r.at[src],
            device_id=(dst, par, orb), device_id_type=MESH)

    def sat_copy(dst, a, b, src):
        return pltpu.make_async_remote_copy(
            src_ref=bucket.at[b * group_orders + a], dst_ref=arrived.at[src],
            send_sem=sat_s.at[dst], recv_sem=sat_r.at[src],
            device_id=(a, par, b), device_id_type=MESH)

    def coef_copy(dst, src):
        return pltpu.make_async_remote_copy(
            src_ref=coef_mine, dst_ref=coefs.at[src],
            send_sem=coef_s.at[dst], recv_sem=coef_r.at[src],
            device_id=(dst, par, orb), device_id_type=MESH)

    def forward():
        return pltpu.make_async_remote_copy(
            src_ref=panels.at[par], dst_ref=panels.at[par],
            send_sem=pair_s.at[0], recv_sem=pair_r.at[0],
            device_id=(lat, other, orb), device_id_type=MESH)

    def backward():
        return pltpu.make_async_remote_copy(
            src_ref=panels.at[par], dst_ref=panels.at[other],
            send_sem=pair_s.at[0], recv_sem=pair_r.at[0],
            device_id=(lat, other, orb), device_id_type=MESH)

    def gram_copy():
        return pltpu.make_async_remote_copy(
            src_ref=gram_send, dst_ref=gram_recv,
            send_sem=pair_s.at[1], recv_sem=pair_r.at[1],
            device_id=(lat, other, orb), device_id_type=MESH)

    def each_lat(action):
        def body(k, c):
            action(lax.rem(lat + k, n_lat))
            return c

        lax.fori_loop(1, n_lat, body, 0)

    def each_src(action):
        def body(k, c):
            action(*peer(k))
            return c

        lax.fori_loop(1, n_src, body, 0)

    loads[0].wait()
    loads[1].wait()
    perm = (iota((width, width), 0)
            == 2 * (iota((width, width), 1) % half) + iota((width, width), 1) // half)
    split_rows = dot_nn(sat_rows[...], perm.astype(F32).astype(BF16)).astype(BF16)
    row = slot_row[...].astype(F32)
    sub = iota((sat_count, sat_count), 0)
    lane = iota((sat_count, sat_count), 1)
    column = jnp.sum(jnp.where(sub == lane, row, 0.0), axis=1, keepdims=True)
    earlier = (column == row) & (sub < lane)
    rank = jnp.sum(jnp.where(earlier, 1.0, 0.0), axis=0, keepdims=True)
    target = row * float(cap) + rank
    pl.semaphore_wait(barrier, n_src)
    each_lat(lambda dst: panel_copy(dst, lat).start())
    step_slots = max(1, min(slots, 512 // cap))

    def fill(i, c):
        spot = (iota((step_slots * cap, sat_count), 0) + i * (step_slots * cap)).astype(F32)
        hot = jnp.where(spot == target, 1.0, 0.0).astype(BF16)
        rows = dot_nn(hot, split_rows).astype(BF16)
        bucket[pl.ds(i * step_slots, step_slots)] = rows.reshape(step_slots, cap, width)
        return c

    if slots == step_slots:
        fill(0, 0)
    else:
        lax.fori_loop(0, slots // step_slots, fill, 0)

    each_src(lambda p, a, b: sat_copy(p, a, b, me).start())
    arrived[me] = bucket[orb * group_orders + lat]
    loads[2].wait()
    loads[3].wait()
    loads[4].wait()

    wide = 2 * group_orders
    line = iota((wide, 1), 0)
    order_col = jnp.zeros((wide, 1), F32)
    for o in range(group_orders):
        order_col = jnp.where(
            lax.rem(line, group_orders) == o, order[0, o].astype(F32), order_col)
    sample = iota((wide, lon), 1).astype(F32)
    x = sample * order_col
    r = x - jnp.floor(x * (1.0 / lon)) * float(lon)
    r = r - jnp.where(iota((wide, lon), 0) >= group_orders, lon / 4.0, 0.0)
    r = r - jnp.floor(r * (1.0 / lon) + 0.5) * float(lon)
    z = (lon / 4.0 - jnp.abs(r)) * (2.0 * math.pi / lon)
    z2 = z * z
    poly = -1.0 / math.factorial(11)
    for d in (9, 7, 5, 3, 1):
        sgn = 1.0 if d % 4 == 1 else -1.0
        poly = poly * z2 + sgn / math.factorial(d)
    trig = poly * z
    high = trig.astype(BF16)
    low = (trig - high.astype(F32)).astype(BF16)
    coef_mine[...] = jnp.zeros_like(coef_mine)
    total_rows = weight.shape[1]
    here = (iota((row_count, total_rows), 1)
            == iota((row_count, total_rows), 0) + lat * row_count)
    scale = math.sqrt(2.0 / lon)
    for h in range(2):
        data = anomaly[h]
        spectrum = (dot_nt(data, high) + dot_nt(data, low)) * scale
        own_weight = jnp.sum(
            jnp.where(here, weight[h:h + 1, :], 0.0), axis=1, keepdims=True)
        coef_mine[:, h * wide:(h + 1) * wide] = (spectrum * own_weight).astype(BF16)
    each_lat(lambda dst: coef_copy(dst, lat).start())
    coefs[lat] = coef_mine[...]

    each_lat(lambda src: panel_copy(src, src).wait_recv())
    forward().start()
    for l in range(n_lat):
        rows = slice(l * row_count, (l + 1) * row_count)
        live = 2 * iota((row_count, half_count), 1) + par <= limit
        left[rows, :] = jnp.where(live, panels[par, l].astype(F32), 0.0).astype(BF16)
    each_lat(lambda src: coef_copy(src, src).wait_recv())
    sign = 1.0 - 2.0 * lax.rem(base + par + order[0, lat], 2).astype(F32)
    products = dot_tn(coefs[...].reshape(total_rows, coefs.shape[2]), left[...])
    place = iota(products.shape, 0)
    for t in range(2):
        spot = t * group_orders + lat
        factor = jnp.where(place == spot, 1.0, jnp.where(place == wide + spot, sign, 0.0))
        right[t] = jnp.sum(products * factor, axis=0, keepdims=True)
    backward().wait_recv()
    for l in range(n_lat):
        rows = slice(l * row_count, (l + 1) * row_count)
        here = (iota((row_count, total_rows), 1)
                == iota((row_count, total_rows), 0) + l * row_count)
        north = jnp.sum(jnp.where(here, weight[0:1, :], 0.0), axis=1, keepdims=True)
        south = jnp.sum(jnp.where(here, weight[1:2, :], 0.0), axis=1, keepdims=True)
        for q in range(2):
            live = 2 * iota((row_count, half_count), 1) + q <= limit
            masked = jnp.where(live, panels[q, l].astype(F32), 0.0)
            factor = jnp.where(par == q, north + south, north - south)
            sides[q, rows, :] = (masked * factor).astype(BF16)

    def grid_tile(i):
        block = left[:, i * half:(i + 1) * half]
        for q in range(2):
            value = dot_tn(block, sides[q])
            for b in range(stripes):
                at = pl.ds(i * half * 2 * stripes + 2 * b + q, half, stride=2 * stripes)
                out[at, :] = value[:, b * LANES:(b + 1) * LANES]

    def save_tile(i):
        span = pl.ds(i * half * 2 * stripes, half * 2 * stripes)
        return pltpu.make_async_copy(out.at[span], out_hbm.at[span], save.at[i])

    tiles = half_count // half
    save_right = pltpu.make_async_copy(right, right_hbm, save.at[tiles])
    save_right.start()
    for i in range(1, tiles):
        grid_tile(i)
        save_tile(i).start()
    each_src(lambda p, a, b: sat_copy(p, a, b, p).wait_recv())

    chunk = max(1, min(n_src, 512 // cap))
    steps = n_src // chunk

    def gram(which):
        cols = pl.ds(pl.multiple_of(which * half, half), half)

        def part(i):
            full = arrived[pl.ds(i * chunk, chunk)].reshape(chunk * cap, width)
            some = arrived[pl.ds(i * chunk, chunk), :, cols].reshape(chunk * cap, half)
            return dot_tn(some, full)

        if steps == 1:
            return part(0)
        return lax.fori_loop(
            0, steps, lambda i, c: c + part(i), jnp.zeros((half, width), F32))

    gram_send[...] = gram(other)
    gram_copy().start()
    own = gram(par)
    grid_tile(0)
    gram_copy().wait_recv()
    summed = own + gram_recv[...]
    for q in range(2):
        for b in range(half // LANES):
            at = pl.ds(2 * b + q, half, stride=2 * stripes)
            keep = ((2 * iota((half, LANES), 0) + par <= limit)
                    & (2 * (iota((half, LANES), 1) + b * LANES) + q <= limit))
            piece = summed[:, q * half + b * LANES:q * half + (b + 1) * LANES]
            out[at, :] = out[at, :] + jnp.where(keep, piece, 0.0)
    save_tile(0).start()
    each_lat(lambda dst: panel_copy(dst, lat).wait_send())
    each_lat(lambda dst: coef_copy(dst, lat).wait_send())
    each_src(lambda p, a, b: sat_copy(p, a, b, me).wait_send())
    forward().wait_send()
    gram_copy().wait_send()
    save_right.wait()
    for i in range(tiles):
        save_tile(i).wait()


def hand_out(flat, side, out, right, sem):
    parts = sem.shape[0] - 1
    rows = flat.shape[0] // parts
    copies = [pltpu.make_async_copy(side, right, sem.at[parts])]
    for i in range(parts):
        span = pl.ds(i * rows, rows)
        copies.append(pltpu.make_async_copy(flat.at[span], out.at[span], sem.at[i]))
    for one in copies:
        one.start()
    for one in copies:
        one.wait()


def shards(sizes, anomaly, row_weight, panel, order_value, deg_first, sat_rows, sat_slot):
    n_lat, n_orb = sizes
    _, group_orders, row_count, _, half_count = panel.shape
    sat_count, width = sat_rows.shape
    half = width // 2
    total = n_lat * row_count
    slots = n_orb * group_orders
    n_src = n_lat * n_orb
    cap = max(16, 2 * sat_count // slots)
    smem = pl.BlockSpec(memory_space=pltpu.SMEM)
    dma = pltpu.SemaphoreType.DMA
    hbm = pl.BlockSpec(memory_space=pltpu.HBM)
    stripes = half_count // LANES
    coef_width = -(-4 * group_orders // LANES) * LANES
    results = (
        jax.ShapeDtypeStruct((half_count * 2 * stripes, LANES), F32),
        jax.ShapeDtypeStruct((2, 1, half_count), F32),
    )
    flat, right = pl.pallas_call(
        functools.partial(exchange_kernel, sizes),
        out_shape=results,
        in_specs=[smem] * 2 + [hbm] * 5,
        out_specs=[hbm] * 2,
        scratch_shapes=[
            pltpu.VMEM(results[0].shape, F32),
            pltpu.VMEM(results[1].shape, F32),
            pltpu.VMEM(anomaly.shape, BF16),
            pltpu.VMEM(row_weight.shape, F32),
            pltpu.VMEM(sat_rows.shape, BF16),
            pltpu.VMEM((1, sat_count), jnp.int32),
            pltpu.VMEM((2, n_lat, row_count, half_count), BF16),
            pltpu.VMEM((n_lat, row_count, coef_width), BF16),
            pltpu.VMEM((slots, cap, width), BF16),
            pltpu.VMEM((n_src, cap, width), BF16),
            pltpu.VMEM((row_count, coef_width), BF16),
            pltpu.VMEM((half, width), F32),
            pltpu.VMEM((half, width), F32),
            pltpu.VMEM((total, half_count), BF16),
            pltpu.VMEM((2, total, half_count), BF16),
            dma((5,)), dma((half_count // half + 1,)),
            dma((n_lat,)), dma((n_lat,)), dma((n_lat,)), dma((n_lat,)),
            dma((n_src,)), dma((n_src,)), dma((2,)), dma((2,)),
        ],
        compiler_params=pltpu.CompilerParams(
            collective_id=0, has_side_effects=True, vmem_limit_bytes=60 * 2**20),
        name="exchange",
    )(
        order_value,
        deg_first,
        anomaly,
        row_weight,
        panel.reshape(group_orders, row_count, half_count),
        sat_rows,
        sat_slot.reshape(1, sat_count),
    )
    flat, right = pl.pallas_call(
        hand_out,
        out_shape=results,
        in_specs=[pl.BlockSpec(memory_space=pl.ANY)] * 2,
        out_specs=[hbm] * 2,
        scratch_shapes=[dma((2 * stripes + 1,))],
        name="hand_out",
    )(flat, right)
    normals = flat.reshape(half_count, stripes, 2, LANES).transpose(0, 2, 1, 3)
    normals = with_layout_constraint(normals, Layout((0, 2, 1, 3)))
    normals = normals.reshape(1, 1, 1, half_count, 2, half_count)
    return normals, right.reshape(1, 1, 2, 1, half_count)


def solution(mesh):
    sizes = (mesh.shape["lat"], mesh.shape["orb"])
    in_specs = (
        P(None, "lat", None),
        P(),
        P("orb", None, "lat", "ord", None),
        P("orb", None),
        P("orb", "lat"),
        P(("lat", "ord", "orb"), None),
        P(("lat", "ord", "orb"), None),
    )
    out_specs = (P("orb", "lat", "ord", None, None, None), P("orb", "lat", None, "ord", None))
    return jax.shard_map(
        functools.partial(shards, sizes), mesh=mesh, in_specs=in_specs,
        out_specs=out_specs, check_vma=False)
```

time: 27.4 us -> 123 us (4.49)
  the two profiles are of different devices: /device:TPU:0 before, /device:TPU:1 now
where the time goes in v2:
time: 123 us; the launch traced here: 122 us
  Pallas kernels  121 us (98%)
  between operations  1.29 us (1%)
    pallas_call x1, Pallas kernels, shards(): pl.pallas_call(hand_out, out_shape=results, in_specs=[pl.BlockSpec(memory...  101 us
    pallas_call x1, Pallas kernels, shards(): pl.pallas_call(functools.partial(exchange_kernel, sizes), out_shape=resul...  20.5 us

profile of v2, /device:TPU:1, one launch (start us, length us, event | category | flops | bytes accessed | tf_op | source)
XLA Modules:
  0.0 122.4 jit_solution(4860323590502037177)
XLA Ops:
  1.3 20.5 %exchange.1 = (f32[6400,128]{1,0:T(8,128)}, f32[2,1,640]{2,1,0:T(1,128)}) custom-call(s32[1,4]{1,0:T(1,128)} %order.1, s32[1,1]{1,0:T(1,128)S(6)} %copy.9.first, bf16[2,16,4320]{2,1,0:T(8,128)(2,1)} %anomaly_hbm.1, f32[2,64]{1,0:T(2,128)} %weight_hbm.1, bf16[4,16,640]{2,1,0:T(8,128)(2,1)} %bitcast.8, bf16[256,256]{1,0:T(8,128)(2,1)} %sat_hbm.1, s32[1,256]{1,0:T(1,128)} %bitcast.9), custom_call_target="tpu_custom_call" | custom-call | tf_op jit(solution)/shard_map/exchange/pallas_call | solution.py:319
  21.7 100.6 %hand_out.1 = (f32[6400,128]{1,0:T(8,128)}, f32[2,1,640]{2,1,0:T(1,128)}) custom-call(f32[6400,128]{1,0:T(8,128)} %get-tuple-element.6.flat, f32[2,1,640]{2,1,0:T(1,128)} %get-tuple-element.7.side), custom_call_target="tpu_custom_call" | custom-call | tf_op jit(solution)/shard_map/hand_out/pallas_call | solution.py:356

commit v3 on v2

--- a/solution.py
+++ b/solution.py
@@ -285,17 +285,26 @@
         save_tile(i).wait()
 
 
-def hand_out(flat, side, out, right, sem):
-    parts = sem.shape[0] - 1
+def hand_out(flat, side, out, right, held, held_side, sem_in, sem_out):
+    parts = sem_in.shape[0] - 1
     rows = flat.shape[0] // parts
-    copies = [pltpu.make_async_copy(side, right, sem.at[parts])]
-    for i in range(parts):
+
+    def pair(i):
+        if i == parts:
+            return (pltpu.make_async_copy(side, held_side, sem_in.at[i]),
+                    pltpu.make_async_copy(held_side, right, sem_out.at[i]))
         span = pl.ds(i * rows, rows)
-        copies.append(pltpu.make_async_copy(flat.at[span], out.at[span], sem.at[i]))
-    for one in copies:
-        one.start()
-    for one in copies:
-        one.wait()
+        return (pltpu.make_async_copy(flat.at[span], held.at[span], sem_in.at[i]),
+                pltpu.make_async_copy(held.at[span], out.at[span], sem_out.at[i]))
+
+    pairs = [pair(i) for i in range(parts + 1)]
+    for fetch, _ in pairs:
+        fetch.start()
+    for fetch, store in pairs:
+        fetch.wait()
+        store.start()
+    for _, store in pairs:
+        store.wait()
 
 
 def shards(sizes, anomaly, row_weight, panel, order_value, deg_first, sat_rows, sat_slot):
@@ -358,7 +367,13 @@
         out_shape=results,
         in_specs=[pl.BlockSpec(memory_space=pl.ANY)] * 2,
         out_specs=[hbm] * 2,
-        scratch_shapes=[dma((2 * stripes + 1,))],
+        scratch_shapes=[
+            pltpu.VMEM(results[0].shape, F32),
+            pltpu.VMEM(results[1].shape, F32),
+            dma((2 * stripes + 1,)),
+            dma((2 * stripes + 1,)),
+        ],
+        compiler_params=pltpu.CompilerParams(vmem_limit_bytes=60 * 2**20),
         name="hand_out",
     )(flat, right)
     normals = flat.reshape(half_count, stripes, 2, LANES).transpose(0, 2, 1, 3)

time: 123 us -> 24.8 us (0.20)
  Pallas kernels: 121 us -> 23.3 us
    pallas_call x1, Pallas kernels: 101 us -> 2.86 us  [shards(): pl.pallas_call(hand_out, out_shape=results, in_specs=[pl.BlockSpec(memory...]
where the time goes in v3:
time: 24.8 us; the launch traced here: 24.6 us
  Pallas kernels  23.3 us (94%)
  between operations  1.29 us (5%)
    pallas_call x1, Pallas kernels, shards(): pl.pallas_call(functools.partial(exchange_kernel, sizes), out_shape=resul...  20.5 us
    pallas_call x1, Pallas kernels, shards(): pl.pallas_call(hand_out, out_shape=results, in_specs=[pl.BlockSpec(memory...  2.86 us

profile of v3, /device:TPU:1, one launch (start us, length us, event | category | flops | bytes accessed | tf_op | source)
XLA Modules:
  0.0 24.6 jit_solution(14488807703407208012)
XLA Ops:
  1.3 20.5 %exchange.1 = (f32[6400,128]{1,0:T(8,128)}, f32[2,1,640]{2,1,0:T(1,128)}) custom-call(s32[1,4]{1,0:T(1,128)} %order.1, s32[1,1]{1,0:T(1,128)S(6)} %copy.9.first, bf16[2,16,4320]{2,1,0:T(8,128)(2,1)} %anomaly_hbm.1, f32[2,64]{1,0:T(2,128)} %weight_hbm.1, bf16[4,16,640]{2,1,0:T(8,128)(2,1)} %bitcast.8, bf16[256,256]{1,0:T(8,128)(2,1)} %sat_hbm.1, s32[1,256]{1,0:T(1,128)} %bitcast.9), custom_call_target="tpu_custom_call" | custom-call | tf_op jit(solution)/shard_map/exchange/pallas_call | solution.py:328
  21.7 2.9 %hand_out.1 = (f32[6400,128]{1,0:T(8,128)}, f32[2,1,640]{2,1,0:T(1,128)}) custom-call(f32[6400,128]{1,0:T(8,128)} %get-tuple-element.6.flat, f32[2,1,640]{2,1,0:T(1,128)} %get-tuple-element.7.side), custom_call_target="tpu_custom_call" | custom-call | tf_op jit(solution)/shard_map/hand_out/pallas_call | solution.py:365

commit v4 on v2

--- a/solution.py
+++ b/solution.py
@@ -35,8 +35,8 @@
 def exchange_kernel(
     sizes,
     order, first, anomaly_hbm, weight_hbm, panel, sat_hbm, slot_hbm,
-    out_hbm, right_hbm,
-    out, right, anomaly, weight, sat_rows, slot_row, panels, coefs,
+    left_hbm, sides_hbm, sat_out, right_hbm,
+    right, anomaly, weight, sat_rows, slot_row, panels, coefs,
     bucket, arrived, coef_mine, gram_send, gram_recv, left, sides,
     load, save, panel_s, panel_r, coef_s, coef_r, sat_s, sat_r, pair_s, pair_r,
 ):
@@ -52,7 +52,6 @@
     par = lax.axis_index("ord")
     orb = lax.axis_index("orb")
     other = 1 - par
-    stripes = half_count // LANES
     base = first[0, 0]
     limit = LMAX - base
     me = lat * n_orb + orb
@@ -204,6 +203,13 @@
         rows = slice(l * row_count, (l + 1) * row_count)
         live = 2 * iota((row_count, half_count), 1) + par <= limit
         left[rows, :] = jnp.where(live, panels[par, l].astype(F32), 0.0).astype(BF16)
+    saves = [
+        pltpu.make_async_copy(right, right_hbm, save.at[0]),
+        pltpu.make_async_copy(left, left_hbm, save.at[1]),
+        pltpu.make_async_copy(sides, sides_hbm, save.at[2]),
+        pltpu.make_async_copy(gram_recv, sat_out, save.at[3]),
+    ]
+    saves[1].start()
     each_lat(lambda src: coef_copy(src, src).wait_recv())
     sign = 1.0 - 2.0 * lax.rem(base + par + order[0, lat], 2).astype(F32)
     products = dot_tn(coefs[...].reshape(total_rows, coefs.shape[2]), left[...])
@@ -212,6 +218,7 @@
         spot = t * group_orders + lat
         factor = jnp.where(place == spot, 1.0, jnp.where(place == wide + spot, sign, 0.0))
         right[t] = jnp.sum(products * factor, axis=0, keepdims=True)
+    saves[0].start()
     backward().wait_recv()
     for l in range(n_lat):
         rows = slice(l * row_count, (l + 1) * row_count)
@@ -225,24 +232,7 @@
             factor = jnp.where(par == q, north + south, north - south)
             sides[q, rows, :] = (masked * factor).astype(BF16)
 
-    def grid_tile(i):
-        block = left[:, i * half:(i + 1) * half]
-        for q in range(2):
-            value = dot_tn(block, sides[q])
-            for b in range(stripes):
-                at = pl.ds(i * half * 2 * stripes + 2 * b + q, half, stride=2 * stripes)
-                out[at, :] = value[:, b * LANES:(b + 1) * LANES]
-
-    def save_tile(i):
-        span = pl.ds(i * half * 2 * stripes, half * 2 * stripes)
-        return pltpu.make_async_copy(out.at[span], out_hbm.at[span], save.at[i])
-
-    tiles = half_count // half
-    save_right = pltpu.make_async_copy(right, right_hbm, save.at[tiles])
-    save_right.start()
-    for i in range(1, tiles):
-        grid_tile(i)
-        save_tile(i).start()
+    saves[2].start()
     each_src(lambda p, a, b: sat_copy(p, a, b, p).wait_recv())
 
     chunk = max(1, min(n_src, 512 // cap))
@@ -264,37 +254,60 @@
     gram_send[...] = gram(other)
     gram_copy().start()
     own = gram(par)
-    grid_tile(0)
     gram_copy().wait_recv()
-    summed = own + gram_recv[...]
-    for q in range(2):
-        for b in range(half // LANES):
-            at = pl.ds(2 * b + q, half, stride=2 * stripes)
-            keep = ((2 * iota((half, LANES), 0) + par <= limit)
-                    & (2 * (iota((half, LANES), 1) + b * LANES) + q <= limit))
-            piece = summed[:, q * half + b * LANES:q * half + (b + 1) * LANES]
-            out[at, :] = out[at, :] + jnp.where(keep, piece, 0.0)
-    save_tile(0).start()
+    spot = iota((half, width), 1)
+    keep = ((2 * iota((half, width), 0) + par <= limit)
+            & (2 * lax.rem(spot, half) + spot // half <= limit))
+    gram_recv[...] = jnp.where(keep, own + gram_recv[...], 0.0)
+    saves[3].start()
     each_lat(lambda dst: panel_copy(dst, lat).wait_send())
     each_lat(lambda dst: coef_copy(dst, lat).wait_send())
     each_src(lambda p, a, b: sat_copy(p, a, b, me).wait_send())
     forward().wait_send()
     gram_copy().wait_send()
-    save_right.wait()
-    for i in range(tiles):
-        save_tile(i).wait()
-
-
-def hand_out(flat, side, out, right, sem):
-    parts = sem.shape[0] - 1
-    rows = flat.shape[0] // parts
-    copies = [pltpu.make_async_copy(side, right, sem.at[parts])]
-    for i in range(parts):
+    for one in saves:
+        one.wait()
+
+
+def normal_kernel(
+    left_hbm, sides_hbm, sat_hbm, right_hbm, out, right_out,
+    left, sides, sat, right, flat, sem_in, sem_out,
+):
+    fetches = [
+        pltpu.make_async_copy(left_hbm, left, sem_in.at[0]),
+        pltpu.make_async_copy(sides_hbm, sides, sem_in.at[1]),
+        pltpu.make_async_copy(sat_hbm, sat, sem_in.at[2]),
+        pltpu.make_async_copy(right_hbm, right, sem_in.at[3]),
+    ]
+    for one in fetches:
+        one.start()
+    half, width = sat.shape
+    half_count = left.shape[1]
+    tiles = half_count // half
+    stripes = half_count // LANES
+    rows = half * 2 * stripes
+    fetches[0].wait()
+    fetches[1].wait()
+    stores = []
+    for i in list(range(1, tiles)) + [0]:
+        if i == 0:
+            fetches[2].wait()
+        block = left[:, i * half:(i + 1) * half]
+        for q in range(2):
+            value = dot_tn(block, sides[q])
+            for b in range(stripes):
+                piece = value[:, b * LANES:(b + 1) * LANES]
+                if i == 0 and b < half // LANES:
+                    at = q * half + b * LANES
+                    piece = piece + sat[:, at:at + LANES]
+                flat[pl.ds(i * rows + 2 * b + q, half, stride=2 * stripes), :] = piece
         span = pl.ds(i * rows, rows)
-        copies.append(pltpu.make_async_copy(flat.at[span], out.at[span], sem.at[i]))
-    for one in copies:
-        one.start()
-    for one in copies:
+        stores.append(pltpu.make_async_copy(flat.at[span], out.at[span], sem_out.at[i]))
+        stores[-1].start()
+    fetches[3].wait()
+    stores.append(pltpu.make_async_copy(right, right_out, sem_out.at[tiles]))
+    stores[-1].start()
+    for one in stores:
         one.wait()
 
 
@@ -312,18 +325,19 @@
     hbm = pl.BlockSpec(memory_space=pltpu.HBM)
     stripes = half_count // LANES
     coef_width = -(-4 * group_orders // LANES) * LANES
-    results = (
-        jax.ShapeDtypeStruct((half_count * 2 * stripes, LANES), F32),
-        jax.ShapeDtypeStruct((2, 1, half_count), F32),
-    )
-    flat, right = pl.pallas_call(
+    tiles = half_count // half
+    left_type = jax.ShapeDtypeStruct((total, half_count), BF16)
+    sides_type = jax.ShapeDtypeStruct((2, total, half_count), BF16)
+    sat_type = jax.ShapeDtypeStruct((half, width), F32)
+    right_type = jax.ShapeDtypeStruct((2, 1, half_count), F32)
+    flat_type = jax.ShapeDtypeStruct((half_count * 2 * stripes, LANES), F32)
+    left, sides, sat, right = pl.pallas_call(
         functools.partial(exchange_kernel, sizes),
-        out_shape=results,
+        out_shape=(left_type, sides_type, sat_type, right_type),
         in_specs=[smem] * 2 + [hbm] * 5,
-        out_specs=[hbm] * 2,
+        out_specs=[hbm] * 4,
         scratch_shapes=[
-            pltpu.VMEM(results[0].shape, F32),
-            pltpu.VMEM(results[1].shape, F32),
+            pltpu.VMEM(right_type.shape, F32),
             pltpu.VMEM(anomaly.shape, BF16),
             pltpu.VMEM(row_weight.shape, F32),
             pltpu.VMEM(sat_rows.shape, BF16),
@@ -337,7 +351,7 @@
             pltpu.VMEM((half, width), F32),
             pltpu.VMEM((total, half_count), BF16),
             pltpu.VMEM((2, total, half_count), BF16),
-            dma((5,)), dma((half_count // half + 1,)),
+            dma((5,)), dma((4,)),
             dma((n_lat,)), dma((n_lat,)), dma((n_lat,)), dma((n_lat,)),
             dma((n_src,)), dma((n_src,)), dma((2,)), dma((2,)),
         ],
@@ -354,13 +368,17 @@
         sat_slot.reshape(1, sat_count),
     )
     flat, right = pl.pallas_call(
-        hand_out,
-        out_shape=results,
-        in_specs=[pl.BlockSpec(memory_space=pl.ANY)] * 2,
+        normal_kernel,
+        out_shape=(flat_type, right_type),
+        in_specs=[pl.BlockSpec(memory_space=pl.ANY)] * 4,
         out_specs=[hbm] * 2,
-        scratch_shapes=[dma((2 * stripes + 1,))],
-        name="hand_out",
-    )(flat, right)
+        scratch_shapes=[
+            pltpu.VMEM(t.shape, t.dtype)
+            for t in (left_type, sides_type, sat_type, right_type, flat_type)
+        ] + [dma((4,)), dma((tiles + 1,))],
+        compiler_params=pltpu.CompilerParams(vmem_limit_bytes=60 * 2**20),
+        name="normal",
+    )(left, sides, sat, right)
     normals = flat.reshape(half_count, stripes, 2, LANES).transpose(0, 2, 1, 3)
     normals = with_layout_constraint(normals, Layout((0, 2, 1, 3)))
     normals = normals.reshape(1, 1, 1, half_count, 2, half_count)

time: 123 us -> 24.2 us (0.20)
  Pallas kernels: 121 us -> 22.8 us
    pallas_call x2, Pallas kernels: 121 us -> 22.8 us  [the longest x1 19.8 us: shards(): pl.pallas_call(functools.partial(exchange_kernel, sizes), out_shape=(left...]
where the time goes in v4:
time: 24.2 us; the launch traced here: 24.1 us
  Pallas kernels  22.8 us (94%)
  between operations  1.29 us (5%)
    pallas_call x1, Pallas kernels, shards(): pl.pallas_call(functools.partial(exchange_kernel, sizes), out_shape=(left...  19.8 us
    pallas_call x1, Pallas kernels, shards(): pl.pallas_call(normal_kernel, out_shape=(flat_type, right_type), in_specs...  3.02 us

profile of v4, /device:TPU:1, one launch (start us, length us, event | category | flops | bytes accessed | tf_op | source)
XLA Modules:
  0.0 24.1 jit_solution(4505023727286459588)
XLA Ops:
  1.3 19.8 %exchange.1 = (bf16[64,640]{1,0:T(8,128)(2,1)}, bf16[2,64,640]{2,1,0:T(8,128)(2,1)}, f32[128,256]{1,0:T(8,128)}, f32[2,1,640]{2,1,0:T(1,128)}) custom-call(s32[1,4]{1,0:T(1,128)} %order.1, s32[1,1]{1,0:T(1,128)S(6)} %copy.9.first, bf16[2,16,4320]{2,1,0:T(8,128)(2,1)} %anomaly_hbm.1, f32[2,64]{1,0:T(2,128)} %weight_hbm.1, bf16[4,16,640]{2,1,0:T(8,128)(2,1)} %bitcast.8, ...), custom_call_target="tpu_custom_call" | custom-call | tf_op jit(solution)/shard_map/exchange/pallas_call | solution.py:334
  21.1 3.0 %normal.1 = (f32[6400,128]{1,0:T(8,128)}, f32[2,1,640]{2,1,0:T(1,128)}) custom-call(bf16[64,640]{1,0:T(8,128)(2,1)} %get-tuple-element.8.left_hbm, bf16[2,64,640]{2,1,0:T(8,128)(2,1)} %get-tuple-element.9.sides_hbm, f32[128,256]{1,0:T(8,128)} %get-tuple-element.10.sat_hbm, f32[2,1,640]{2,1,0:T(1,128)} %get-tuple-element.11.right_hbm), custom_call_target="tpu_custom_call" | custom-call | tf_op jit(solution)/shard_map/normal/pallas_call | solution.py:370

commit v5 on v4

--- a/solution.py
+++ b/solution.py
@@ -141,8 +141,6 @@
     earlier = (column == row) & (sub < lane)
     rank = jnp.sum(jnp.where(earlier, 1.0, 0.0), axis=0, keepdims=True)
     target = row * float(cap) + rank
-    pl.semaphore_wait(barrier, n_src)
-    each_lat(lambda dst: panel_copy(dst, lat).start())
     step_slots = max(1, min(slots, 512 // cap))
 
     def fill(i, c):
@@ -157,6 +155,8 @@
     else:
         lax.fori_loop(0, slots // step_slots, fill, 0)
 
+    pl.semaphore_wait(barrier, n_src)
+    each_lat(lambda dst: panel_copy(dst, lat).start())
     each_src(lambda p, a, b: sat_copy(p, a, b, me).start())
     arrived[me] = bucket[orb * group_orders + lat]
     loads[2].wait()

time: 24.2 us -> 24.2 us (level)
  no operation moved by 1% of the time
where the time goes in v5:
time: 24.2 us; the launch traced here: 24.1 us
  Pallas kernels  22.8 us (94%)
  between operations  1.29 us (5%)
    pallas_call x1, Pallas kernels, shards(): pl.pallas_call(functools.partial(exchange_kernel, sizes), out_shape=(left...  19.8 us
    pallas_call x1, Pallas kernels, shards(): pl.pallas_call(normal_kernel, out_shape=(flat_type, right_type), in_specs...  3.02 us

profile of v5, /device:TPU:1, one launch (start us, length us, event | category | flops | bytes accessed | tf_op | source)
XLA Modules:
  0.0 24.1 jit_solution(16269793518105409310)
XLA Ops:
  1.3 19.8 %exchange.1 = (bf16[64,640]{1,0:T(8,128)(2,1)}, bf16[2,64,640]{2,1,0:T(8,128)(2,1)}, f32[128,256]{1,0:T(8,128)}, f32[2,1,640]{2,1,0:T(1,128)}) custom-call(s32[1,4]{1,0:T(1,128)} %order.1, s32[1,1]{1,0:T(1,128)S(6)} %copy.9.first, bf16[2,16,4320]{2,1,0:T(8,128)(2,1)} %anomaly_hbm.1, f32[2,64]{1,0:T(2,128)} %weight_hbm.1, bf16[4,16,640]{2,1,0:T(8,128)(2,1)} %bitcast.8, ...), custom_call_target="tpu_custom_call" | custom-call | tf_op jit(solution)/shard_map/exchange/pallas_call | solution.py:334
  21.1 3.0 %normal.1 = (f32[6400,128]{1,0:T(8,128)}, f32[2,1,640]{2,1,0:T(1,128)}) custom-call(bf16[64,640]{1,0:T(8,128)(2,1)} %get-tuple-element.8.left_hbm, bf16[2,64,640]{2,1,0:T(8,128)(2,1)} %get-tuple-element.9.sides_hbm, f32[128,256]{1,0:T(8,128)} %get-tuple-element.10.sat_hbm, f32[2,1,640]{2,1,0:T(1,128)} %get-tuple-element.11.right_hbm), custom_call_target="tpu_custom_call" | custom-call | tf_op jit(solution)/shard_map/normal/pallas_call | solution.py:370
